TPU v7x, 32 devices: a whole 2x2x4 slice. The times are simulated.
32 devices in a mesh: grp: 4 (over z), seq: 8 (over y, x, core).
Axes of the slice: x: 2, y: 2, z: 4, core: 2. Of those that a mesh axis runs over, the one named last changes fastest.
Arguments:
- long_x: bfloat16 [4, 1024, 768], P('grp', 'seq'), may hold values from -6 to 6
- short_x: bfloat16 [128, 256, 768], P(('grp', 'seq')), may hold values from -6 to 6
- long_dy: bfloat16 [4, 1024, 768], P('grp', 'seq'), may hold values from -6 to 6
- short_dy: bfloat16 [128, 256, 768], P(('grp', 'seq')), may hold values from -6 to 6
- short_live: int32 [32], P(('grp', 'seq')), may hold values from 0 to 4, as said below
- query_weight: bfloat16 [768, 768], replicated, may hold values from -0.21875 to 0.21875
- key_weight: bfloat16 [768, 768], replicated, may hold values from -0.21875 to 0.21875
- value_weight: bfloat16 [768, 768], replicated, may hold values from -0.21875 to 0.21875
- out_weight: bfloat16 [768, 768], replicated, may hold values from -0.4375 to 0.4375
- up_weight: bfloat16 [768, 3072], replicated, may hold values from -0.21875 to 0.21875
- down_weight: bfloat16 [3072, 768], replicated, may hold values from -0.109375 to 0.109375
- length_proj: bfloat16 [256, 1024], replicated, may hold values from -0.25 to 0.25
- gain_one: float32 [768], replicated, may hold values from 0.5 to 1.5
- shift_one: float32 [768], replicated, may hold values from -1.5 to 1.5
- gain_two: float32 [768], replicated, may hold values from 0.5 to 1.5
- shift_two: float32 [768], replicated, may hold values from -1.5 to 1.5
Outputs:
- long_out: bfloat16 [4, 1024, 768], P('grp', 'seq')
- short_out: bfloat16 [128, 256, 768], P(('grp', 'seq'))
- long_grad: bfloat16 [4, 1024, 768], P('grp', 'seq')
- short_grad: bfloat16 [128, 256, 768], P(('grp', 'seq'))
- query_grad: float32 [768, 768], P(('grp', 'seq'))
- key_grad: float32 [768, 768], P(('grp', 'seq'))
- value_grad: float32 [768, 768], P(('grp', 'seq'))
- out_grad: float32 [768, 768], P(('grp', 'seq'))
- up_grad: float32 [768, 3072], P(('grp', 'seq'))
- down_grad: float32 [3072, 768], P(('grp', 'seq'))
- proj_grad: float32 [256, 1024], P('grp', 'seq')
- gain_one_grad: float32 [768], P(('grp', 'seq'))
- shift_one_grad: float32 [768], P(('grp', 'seq'))
- gain_two_grad: float32 [768], P(('grp', 'seq'))
- shift_two_grad: float32 [768], P(('grp', 'seq'))
Inputs may be any that keep to these rules, and one draw needn't show every extreme that they name: `short_live`: some device has all 4 short items live and some device has none.
All inputs are finite; a program needn't handle non-finite values.
Results may differ from a plain program's by a relative error of at most 0.033.
Values may be sent and summed in bfloat16 or wider, within the bound.
A program may use at most 256 MiB of HBM per device.

v0:
```python
import functools

import jax
import jax.numpy as jnp
from jax import lax
from jax.experimental import pallas as pl
from jax.experimental.pallas import tpu as pltpu
from jax.sharding import PartitionSpec as P

HD = 64
KP = 256


norm_eps = 1e-05


def shortened(shard):
    return jax.tree.map(lambda a: a.astype(jnp.bfloat16) if a.dtype == jnp.float32 else a, shard)


def norm_rows(resid, gain_vec, shift_vec):
    row_mean = jnp.mean(resid, axis=-1, keepdims=True)
    centred = resid - row_mean
    variance = jnp.mean(centred * centred, axis=-1, keepdims=True)
    return centred * lax.rsqrt(variance + norm_eps) * gain_vec + shift_vec


def smooth_gate(upward):
    return jax.nn.gelu(upward, approximate=True)


def same_sums(partials):
    return partials


def layer_pass(sequences, cotangent, live_rows, proj_cols, fold_summaries, fold_grads, params):
    (
        query_w,
        key_w,
        value_w,
        out_w,
        up_w,
        down_w,
        gain_first,
        shift_first,
        gain_second,
        shift_second,
    ) = params
    seq_count, length, model_width = sequences.shape
    head_count = model_width // HD
    wide = jnp.float32
    narrow = jnp.bfloat16
    queries = (
        0.125 * jnp.einsum("nld,de->nle", sequences, query_w, preferred_element_type=wide)
    ).astype(narrow)
    key_vecs = jnp.einsum("nld,de->nle", sequences, key_w, preferred_element_type=wide).astype(
        narrow
    )
    value_vecs = jnp.einsum("nld,de->nle", sequences, value_w, preferred_element_type=wide).astype(
        narrow
    )
    key_part = jnp.einsum("kl,nld->nkd", proj_cols, key_vecs, preferred_element_type=wide)
    value_part = jnp.einsum("kl,nld->nkd", proj_cols, value_vecs, preferred_element_type=wide)
    key_sum, value_sum = fold_summaries((key_part, value_part))
    key_heads = key_sum.astype(narrow).reshape(seq_count, KP, head_count, HD)
    value_heads = value_sum.astype(narrow).reshape(seq_count, KP, head_count, HD)
    query_heads = queries.reshape(seq_count, length, head_count, HD)
    scores = jnp.einsum("nlhe,nkhe->nhlk", query_heads, key_heads, preferred_element_type=wide)
    attn_probs = jax.nn.softmax(scores, axis=-1)
    probs_low = attn_probs.astype(narrow)
    mixed_heads = (
        jnp.einsum("nhlk,nkhe->nlhe", probs_low, value_heads, preferred_element_type=wide)
        .reshape(seq_count, length, model_width)
        .astype(narrow)
    )
    attn_out = jnp.einsum("nld,de->nle", mixed_heads, out_w, preferred_element_type=wide)
    hidden, first_back = jax.vjp(
        norm_rows, sequences.astype(wide) + attn_out, gain_first, shift_first
    )
    hidden_low = hidden.astype(narrow)
    upward = jnp.einsum("nld,df->nlf", hidden_low, up_w, preferred_element_type=wide)
    activated, gate_back = jax.vjp(smooth_gate, upward)
    activated_low = activated.astype(narrow)
    branch = jnp.einsum("nlf,fd->nld", activated_low, down_w, preferred_element_type=wide)
    normed, second_back = jax.vjp(norm_rows, hidden + branch, gain_second, shift_second)
    result = normed * live_rows[:, None, None]
    grad_top = cotangent.astype(wide) * live_rows[:, None, None]
    grad_resid_two, grad_gain_two, grad_shift_two = second_back(grad_top)
    grad_branch = grad_resid_two.astype(narrow)
    grad_down = jnp.einsum("nlf,nld->fd", activated_low, grad_branch, preferred_element_type=wide)
    grad_activated = jnp.einsum("nld,fd->nlf", grad_branch, down_w, preferred_element_type=wide)
    (grad_upward,) = gate_back(grad_activated)
    grad_upward_low = grad_upward.astype(narrow)
    grad_up = jnp.einsum("nld,nlf->df", hidden_low, grad_upward_low, preferred_element_type=wide)
    grad_hidden = grad_resid_two + jnp.einsum(
        "nlf,df->nld", grad_upward_low, up_w, preferred_element_type=wide
    )
    grad_resid_one, grad_gain_one, grad_shift_one = first_back(grad_hidden)
    grad_attn = grad_resid_one.astype(narrow)
    grad_out = jnp.einsum("nld,nle->de", mixed_heads, grad_attn, preferred_element_type=wide)
    grad_mixed = (
        jnp.einsum("nle,de->nld", grad_attn, out_w, preferred_element_type=wide)
        .astype(narrow)
        .reshape(seq_count, length, head_count, HD)
    )
    grad_probs = jnp.einsum("nlhe,nkhe->nhlk", grad_mixed, value_heads, preferred_element_type=wide)
    value_grad_part = jnp.einsum(
        "nhlk,nlhe->nkhe", probs_low, grad_mixed, preferred_element_type=wide
    ).reshape(seq_count, KP, model_width)
    grad_scores = attn_probs * (
        grad_probs - jnp.sum(grad_probs * attn_probs, axis=-1, keepdims=True)
    )
    scores_low = grad_scores.astype(narrow)
    grad_queries = (
        jnp.einsum("nhlk,nkhe->nlhe", scores_low, key_heads, preferred_element_type=wide).astype(
            narrow
        )
        * 0.125
    ).reshape(seq_count, length, model_width)
    key_grad_part = jnp.einsum(
        "nhlk,nlhe->nkhe", scores_low, query_heads, preferred_element_type=wide
    ).reshape(seq_count, KP, model_width)
    key_grad_sum, value_grad_sum = fold_grads((key_grad_part, value_grad_part))
    key_grad_low = key_grad_sum.astype(narrow)
    value_grad_low = value_grad_sum.astype(narrow)
    grad_keys = jnp.einsum(
        "kl,nkd->nld", proj_cols, key_grad_low, preferred_element_type=wide
    ).astype(narrow)
    grad_values = jnp.einsum(
        "kl,nkd->nld", proj_cols, value_grad_low, preferred_element_type=wide
    ).astype(narrow)
    grad_cols = jnp.einsum(
        "nkd,nld->kl", key_grad_low, key_vecs, preferred_element_type=wide
    ) + jnp.einsum("nkd,nld->kl", value_grad_low, value_vecs, preferred_element_type=wide)
    grad_query = jnp.einsum("nld,nle->de", sequences, grad_queries, preferred_element_type=wide)
    grad_key = jnp.einsum("nld,nle->de", sequences, grad_keys, preferred_element_type=wide)
    grad_value = jnp.einsum("nld,nle->de", sequences, grad_values, preferred_element_type=wide)
    grad_sequences = grad_resid_one + jnp.einsum(
        "nle,de->nld", grad_queries, query_w, preferred_element_type=wide
    )
    grad_sequences = grad_sequences + jnp.einsum(
        "nle,de->nld", grad_keys, key_w, preferred_element_type=wide
    )
    grad_sequences = grad_sequences + jnp.einsum(
        "nle,de->nld", grad_values, value_w, preferred_element_type=wide
    )
    weight_grads = (
        grad_query,
        grad_key,
        grad_value,
        grad_out,
        grad_up,
        grad_down,
        grad_gain_one,
        grad_shift_one,
        grad_gain_two,
        grad_shift_two,
    )
    return (result, grad_sequences, weight_grads, grad_cols)


def shards(
    long_x,
    short_x,
    long_dy,
    short_dy,
    short_live,
    query_weight,
    key_weight,
    value_weight,
    out_weight,
    up_weight,
    down_weight,
    length_proj,
    gain_one,
    shift_one,
    gain_two,
    shift_two,
):
    params = (
        query_weight,
        key_weight,
        value_weight,
        out_weight,
        up_weight,
        down_weight,
        gain_one,
        shift_one,
        gain_two,
        shift_two,
    )
    shard_len = long_x.shape[1]
    slot_count = short_x.shape[0]
    short_len = short_x.shape[1]
    shard_start = lax.axis_index("seq") * shard_len
    long_cols = lax.dynamic_slice_in_dim(length_proj, shard_start, shard_len, 1)

    def sum_summaries(partials):
        return jax.tree.map(
            lambda part: part.astype(jnp.float32), lax.psum(shortened(partials), "seq")
        )

    def sum_summary_grads(partials):
        return jax.tree.map(
            lambda part: part.astype(jnp.float32), lax.psum(shortened(partials), "seq")
        )

    long_live = jnp.ones((long_x.shape[0],), jnp.float32)
    long_result, long_back, long_weights, long_proj = layer_pass(
        long_x, long_dy, long_live, long_cols, sum_summaries, sum_summary_grads, params
    )
    short_mask = (jnp.arange(slot_count) < short_live[0]).astype(jnp.float32)
    short_result, short_back, short_weights, short_proj = layer_pass(
        short_x, short_dy, short_mask, length_proj[:, :short_len], same_sums, same_sums, params
    )
    summed = jax.tree.map(jnp.add, long_weights, short_weights)
    (
        grad_query,
        grad_key,
        grad_value,
        grad_out,
        grad_up,
        grad_down,
        grad_gain_one,
        grad_shift_one,
        grad_gain_two,
        grad_shift_two,
    ) = summed
    proj_total = jnp.zeros(length_proj.shape, jnp.float32)
    proj_total = lax.dynamic_update_slice_in_dim(proj_total, long_proj, shard_start, 1)
    proj_total = proj_total.at[:, :short_len].add(short_proj)
    proj_rows = lax.psum_scatter(
        proj_total.astype(jnp.bfloat16), "grp", scatter_dimension=0, tiled=True
    )
    proj_part = lax.psum_scatter(proj_rows, "seq", scatter_dimension=1, tiled=True).astype(
        jnp.float32
    )
    reduced = (
        lax.psum_scatter(grad_query, ("grp", "seq"), scatter_dimension=0, tiled=True),
        lax.psum_scatter(grad_key, ("grp", "seq"), scatter_dimension=0, tiled=True),
        lax.psum_scatter(grad_value, ("grp", "seq"), scatter_dimension=0, tiled=True),
        lax.psum_scatter(grad_out, ("grp", "seq"), scatter_dimension=0, tiled=True),
        lax.psum_scatter(grad_up, ("grp", "seq"), scatter_dimension=0, tiled=True),
        lax.psum_scatter(grad_down, ("grp", "seq"), scatter_dimension=0, tiled=True),
        lax.psum_scatter(grad_gain_one, ("grp", "seq"), scatter_dimension=0, tiled=True),
        lax.psum_scatter(grad_shift_one, ("grp", "seq"), scatter_dimension=0, tiled=True),
        lax.psum_scatter(grad_gain_two, ("grp", "seq"), scatter_dimension=0, tiled=True),
        lax.psum_scatter(grad_shift_two, ("grp", "seq"), scatter_dimension=0, tiled=True),
    )
    reduced = tuple(reduced)
    return (
        (
            long_result.astype(jnp.bfloat16),
            short_result.astype(jnp.bfloat16),
            long_back.astype(jnp.bfloat16),
            short_back.astype(jnp.bfloat16),
        )
        + reduced[:6]
        + (proj_part,)
        + reduced[6:]
    )


MESH_ID = pl.DeviceIdType.MESH
BF = jnp.bfloat16
F32 = jnp.float32
VMEM_BYTES = 65400 * 1024
GELU_A = 0.7978845608028654
GELU_B = 0.044715 * GELU_A
SEQ = 8


def mm(a, b, ca=1, cb=0):
    return lax.dot_general(a, b, (((ca,), (cb,)), ((), ())), preferred_element_type=F32)


def span(start, size, step=None):
    return pl.ds(pl.multiple_of(start, step or size), size)


def here():
    return lax.axis_index("grp"), lax.axis_index("seq")


def greet(peers):
    barrier = pltpu.get_barrier_semaphore()
    for peer in peers:
        pl.semaphore_signal(barrier, inc=1, device_id=peer, device_id_type=MESH_ID)
    pl.semaphore_wait(barrier, len(peers))


def seq_peers():
    g, s = here()
    return [(g, lax.rem(s + k, SEQ)) for k in range(1, SEQ)]


def grp_peers(groups):
    g, s = here()
    return [(lax.rem(g + k, groups), s) for k in range(1, groups)]


class Exchange:
    def __init__(self, part, got_core, got, full, send_sem, recv_sem):
        self.part, self.got_core, self.got, self.full = part, got_core, got, full
        self.send_sem, self.recv_sem = send_sem, recv_sem

    def place(self):
        _, s = here()
        core, chip = lax.rem(s, 2), lax.div(s, 2)
        x, y = 1 - 2 * lax.rem(chip, 2), 2 - 4 * lax.div(chip, 2)
        return core, chip, (chip + x, chip + y, chip + x + y)

    def send(self, n, src, dst, to):
        g, _ = here()
        return pltpu.make_async_remote_copy(
            src_ref=src,
            dst_ref=dst,
            send_sem=self.send_sem.at[n],
            recv_sem=self.recv_sem.at[n],
            device_id=(g, to),
            device_id_type=MESH_ID,
        )

    def halve(self):
        core, chip, _ = self.place()
        return self.send(0, self.part.at[pl.ds(4 * (1 - core), 4)], self.got_core, 2 * chip + 1 - core)

    def across(self):
        core, _, chips = self.place()
        return [
            self.send(1 + k, self.part.at[4 * core + to], self.got.at[k], 2 * to + core) for k, to in enumerate(chips)
        ]

    def spread(self):
        core, chip, chips = self.place()
        own = self.full.at[4 * core + chip]
        return [self.send(4 + k, own, own, 2 * to + core) for k, to in enumerate(chips)]

    def join(self):
        core, chip, _ = self.place()
        own = self.full.at[pl.ds(4 * core, 4)]
        return self.send(7, own, own, 2 * chip + 1 - core)

    def start(self):
        self.halve().start()

    def first(self):
        core, _, _ = self.place()
        self.halve().wait_recv()
        for n in range(4):
            self.part[4 * core + n] = (self.part[4 * core + n].astype(F32) + self.got_core[n].astype(F32)).astype(BF)
        for c in self.across():
            c.start()

    def second(self):
        core, chip, _ = self.place()
        for c in self.across():
            c.wait_recv()
        total = self.part[4 * core + chip].astype(F32)
        for k in range(3):
            total += self.got[k].astype(F32)
        self.full[4 * core + chip] = total.astype(BF)
        for c in self.spread():
            c.start()

    def third(self):
        for c in self.spread():
            c.wait_recv()
        self.join().start()

    def finish(self):
        self.join().wait_recv()

    def close(self):
        for c in [self.halve()] + self.across() + self.spread() + [self.join()]:
            c.wait_send()


def exchange_scratch(rows, width):
    shapes = [(SEQ, rows, width), (4, rows, width), (3, rows, width), (SEQ, rows, width)]
    return [pltpu.VMEM(a, BF) for a in shapes] + [pltpu.SemaphoreType.DMA((8,)) for _ in range(4)]


def halves(block):
    low_lane = lax.broadcasted_iota(jnp.int32, block.shape, 1) < HD
    zero = jnp.zeros_like(block)
    return jnp.concatenate([jnp.where(low_lane, block, zero), jnp.where(low_lane, zero, block)], 0)


def unhalve(block):
    n = block.shape[0] // 2
    low_lane = lax.broadcasted_iota(jnp.int32, (n, block.shape[1]), 1) < HD
    return jnp.where(low_lane, block[:n], block[n:])


def norm_stats(v):
    mean = jnp.mean(v, -1, keepdims=True)
    centred = v - mean
    root = lax.rsqrt(jnp.mean(centred * centred, -1, keepdims=True) + norm_eps)
    return centred * root, root


def norm_back(grad, gain, xhat, root):
    gg = grad * gain
    return (gg - jnp.mean(gg, -1, keepdims=True) - xhat * jnp.mean(gg * xhat, -1, keepdims=True)) * root


def fold_rows(v):
    return jnp.sum(v.reshape(v.shape[0] // 8, 8, v.shape[1]), 0)


def gelu_pair(u):
    u2 = u * u
    s = 0.5 + 0.5 * jnp.tanh(u * (GELU_A + GELU_B * u2))
    a = u * s
    return a, s + a * (1.0 - s) * (2.0 * GELU_A + 6.0 * GELU_B * u2)


def places(groups):
    out = []
    for d in range(groups * SEQ):
        z, y, x, c = d // SEQ, (d // 4) % 2, (d // 2) % 2, d % 2
        out.append((((x * 2 + y) * groups + z, c), ((y * 2 + x) * groups + z, c)))
    return out


class Scatter:
    def __init__(self, src, base, bits, recv0, recv1, recv2, last, send_sem, recv_sem, send_z, recv_z):
        self.src, self.base, self.bits = src, base, bits
        self.recv, self.last = (recv0, recv1, recv2), last
        self.rows, self.lanes = last.shape[1:]
        self.send_sem, self.recv_sem, self.send_z, self.recv_z = send_sem, recv_sem, send_z, recv_z

    def mine(self, n):
        _, s = here()
        return lax.rem(lax.div(s, self.bits[n]), 2)

    def half(self, n, which):
        size = self.recv[n].shape[0]
        if n == 0:
            return self.src, self.base, which * self.lanes
        return self.recv[n - 1], which * size, 0

    def hop(self, n):
        g, s = here()
        mine, bit = self.mine(n), self.bits[n]
        src, row, lane = self.half(n, 1 - mine)
        size = self.recv[n].shape[0]
        return pltpu.make_async_remote_copy(
            src_ref=src.at[span(row, size, self.rows), span(lane, self.lanes, 128)],
            dst_ref=self.recv[n],
            send_sem=self.send_sem.at[n],
            recv_sem=self.recv_sem.at[n],
            device_id=(g, s + bit - 2 * bit * mine),
            device_id_type=MESH_ID,
        )

    def along(self):
        g, s = here()
        groups = self.last.shape[0] + 1
        out = []
        for k in range(1, groups):
            to = lax.rem(g + k, groups)
            out.append(
                pltpu.make_async_remote_copy(
                    src_ref=self.recv[2].at[span(to * self.rows, self.rows)],
                    dst_ref=self.last.at[k - 1],
                    send_sem=self.send_z.at[k - 1],
                    recv_sem=self.recv_z.at[k - 1],
                    device_id=(to, s),
                    device_id_type=MESH_ID,
                )
            )
        return out

    def start(self):
        self.hop(0).start()

    def step(self, n):
        src, row, lane = self.half(n, self.mine(n))
        self.hop(n).wait_recv()
        dst = self.recv[n]
        block = 2 * self.rows

        @pl.loop(0, dst.shape[0] // block)
        def _(i):
            to, at = span(i * block, block), span(row + i * block, block, self.rows)
            dst[to, :] = (dst[to, :].astype(F32) + src[at, span(lane, self.lanes, 128)].astype(F32)).astype(BF)

        if n < 2:
            self.hop(n + 1).start()
        else:
            for c in self.along():
                c.start()

    def total(self, out, row, column):
        for c in self.along():
            c.wait_recv()
        g, _ = here()
        total = self.recv[2][span(g * self.rows, self.rows), :].astype(F32)
        for k in range(self.last.shape[0]):
            total += self.last[k].astype(F32)
        few = self.rows // 2
        out[row : row + few, column : column + self.lanes] = total[:few]
        out[row : row + few, column + self.lanes : column + 2 * self.lanes] = total[few:]

    def close(self):
        for n in range(3):
            self.hop(n).wait_send()
        for c in self.along():
            c.wait_send()


class Place:
    def __init__(self, ref, row):
        self.ref, self.row = ref, row

    def __add__(self, rows):
        return Place(self.ref, self.row + rows)


def window(place, size, step=None):
    row = place.row
    rows = pl.ds(row, size) if isinstance(row, int) else span(row, size, step)
    return place.ref, rows


class Arena:
    def __getitem__(self, key):
        (ref, rows), lanes = key
        return ref[rows, lanes]

    def __setitem__(self, key, value):
        (ref, rows), lanes = key
        ref[rows, lanes] = value


class Vectors:
    def __init__(self, mine, recv, last, send_sem, recv_sem, send_z, recv_z):
        self.mine, self.recv, self.last = mine, recv, last
        self.sems = (send_sem, recv_sem, send_z, recv_z)

    def hop(self, n):
        g, s = here()
        bit = 1 << n
        other = s + bit - 2 * bit * lax.rem(lax.div(s, bit), 2)
        return pltpu.make_async_remote_copy(
            src_ref=self.mine.at[n],
            dst_ref=self.recv.at[n],
            send_sem=self.sems[0].at[n],
            recv_sem=self.sems[1].at[n],
            device_id=(g, other),
            device_id_type=MESH_ID,
        )

    def along(self):
        g, s = here()
        groups = self.last.shape[0] + 1
        return [
            pltpu.make_async_remote_copy(
                src_ref=self.mine.at[3],
                dst_ref=self.last.at[k - 1],
                send_sem=self.sems[2].at[k - 1],
                recv_sem=self.sems[3].at[k - 1],
                device_id=(lax.rem(g + k, groups), s),
                device_id_type=MESH_ID,
            )
            for k in range(1, groups)
        ]

    def start(self):
        self.hop(0).start()

    def step(self, n):
        self.hop(n).wait_recv()
        self.mine[n + 1] = self.mine[n] + self.recv[n]
        if n < 2:
            self.hop(n + 1).start()
        else:
            for c in self.along():
                c.start()

    def total(self):
        for c in self.along():
            c.wait_recv()
        return self.mine[3] + sum(self.last[k] for k in range(self.last.shape[0]))

    def close(self):
        for c in [self.hop(n) for n in range(3)] + self.along():
            c.wait_send()


class ProjGrad:
    def __init__(self, part, got, short, got_short, *sems):
        self.part, self.got, self.short, self.got_short, self.sems = part, got, short, got_short, sems

    def along(self, first, size):
        g, s = here()
        groups = self.part.shape[0]
        send, recv = self.sems[:2] if first == 0 else self.sems[2:4]
        out = []
        for k in range(1, groups):
            to = lax.rem(g + k, groups)
            out.append(
                pltpu.make_async_remote_copy(
                    src_ref=self.part.at[to, :, pl.ds(first, size)],
                    dst_ref=self.got.at[k - 1, :, pl.ds(first, size)],
                    send_sem=send.at[k - 1],
                    recv_sem=recv.at[k - 1],
                    device_id=(to, s),
                    device_id_type=MESH_ID,
                )
            )
        return out

    def across(self, b):
        g, s = here()
        slot = lax.rem(s - b + 2 * SEQ - 1, SEQ)
        return pltpu.make_async_remote_copy(
            src_ref=self.short.at[b],
            dst_ref=self.got_short.at[slot],
            send_sem=self.sems[4].at[b],
            recv_sem=self.sems[5].at[slot],
            device_id=(g, jnp.int32(b)),
            device_id_type=MESH_ID,
        )

    def arrived(self, slot):
        g, s = here()
        return pltpu.make_async_remote_copy(
            src_ref=self.short.at[0],
            dst_ref=self.got_short.at[slot],
            send_sem=self.sems[4].at[0],
            recv_sem=self.sems[5].at[slot],
            device_id=(g, s),
            device_id_type=MESH_ID,
        )

    def start(self, first, size):
        for c in self.along(first, size):
            c.start()

    def summed(self, first, size):
        g, _ = here()
        for c in self.along(first, size):
            c.wait_recv()
        total = self.part[g, :, first : first + size].astype(F32)
        for k in range(self.got.shape[0]):
            total += self.got[k, :, first : first + size].astype(F32)
        return total

    def across_all(self, shard, short_len):
        _, s = here()
        total = self.summed(shard, short_len)
        for b in range(self.short.shape[0]):
            self.short[b] = total[:, b * shard : (b + 1) * shard].astype(BF)

            @pl.when(s != b)
            def _(b=b):
                self.across(b).start()

    def finish(self, out, shard):
        _, s = here()
        count = self.short.shape[0]
        out[...] = self.summed(0, shard)

        @pl.when(s < count)
        def _():
            total = out[...] + self.short[lax.rem(s, count)].astype(F32)
            for slot in range(SEQ - 1):
                self.arrived(slot).wait_recv()
                total += self.got_short[slot].astype(F32)
            out[...] = total

    def close(self):
        _, s = here()
        shard = self.short.shape[2]
        for c in self.along(0, shard) + self.along(shard, self.part.shape[2] - shard):
            c.wait_send()
        for b in range(self.short.shape[0]):

            @pl.when(s != b)
            def _(b=b):
                self.across(b).wait_send()


def layer_kernel(slots, groups, shard, *refs):
    refs = list(refs)

    def take(n):
        out = refs[:n]
        del refs[:n]
        return out

    (long_x, short_x, long_dy, short_dy, live) = take(5)
    (wq_in, wk_in, wv_in, wo_in, up_in, down_in, proj) = take(7)
    (gain1, shift1, gain2, shift2) = (a[...].reshape(1, -1) for a in take(4))
    (long_out, short_out, long_grad, short_grad) = take(4)
    (grad_q, grad_k, grad_v, grad_o, grad_up, grad_down, grad_proj, vec_out) = take(8)
    (q_hbm, y_hbm, mixed_hbm, probs_hbm, sums_hbm) = take(5)
    (a_ref, s_ref, ud_ref, x_ref, m_ref, h_ref, w_ref, p_ref, b_ref, resid, root, vec, pcols, pshort, pacc) = take(15)
    (sem_in, sem_out, sem_back) = take(3)
    exch_bufs = take(4)
    forward_exchange = Exchange(*exch_bufs, *take(2))
    backward_exchange = Exchange(*exch_bufs, *take(2))
    vectors = Vectors(*take(7))
    projected = ProjGrad(*take(10))

    g, s = here()
    short_len = short_x.shape[1]
    width = resid.shape[1]
    wide = 4 * width
    shorts = slots * short_len
    tokens = shorts + shard
    devices = groups * SEQ
    few = width // devices
    lanes = width // 2
    act, slope = Place(a_ref, 0), Place(s_ref, 0)
    up, down = Place(ud_ref, 0), Place(ud_ref, wide)
    xs, ms, hs, xhs = Place(x_ref, 0), Place(m_ref, 0), Place(h_ref, 0), Place(h_ref, tokens)
    wo, pack, weights = Place(w_ref, 0), Place(p_ref, 0), Place(h_ref, 0)
    pack_up = act
    q1, y1 = act, act + tokens
    probs1, sums1 = Place(s_ref, 0), Place(p_ref, 0)
    q2, y2 = slope, slope + tokens
    long_sums2 = y2 + (slots + 1) * KP
    key_grads = long_sums2 + 2 * KP
    probs2, through = Place(ud_ref, 0), Place(ud_ref, 0)
    sums2, gq2 = pack + width, pack_up + 4 * width
    value_grads, ms2, x2s = Place(b_ref, 0), hs, ms

    orders = ((1, 2, 4), (1, 4, 2))

    def unit(base, order):
        return Scatter(base.ref, base.row, orders[order], *take(8))

    downs = [unit(pack + n * width, n % 2) for n in range(4)]
    ups = [unit(pack_up + n * width, n % 2) for n in range(4)]
    unit_o, unit_q, unit_v, unit_k = (unit(pack + n * width, n % 2) for n in range(4))
    assert not refs

    copy = pltpu.make_async_copy
    at = lambda place, size: place.ref.at[pl.ds(place.row, size)]
    arena = Arena()
    counts = {"in": 0, "out": 0, "back": 0}

    def move(kind, a, b):
        sem = {"in": sem_in, "out": sem_out, "back": sem_back}[kind]
        counts[kind] += 1
        return copy(a, b, sem.at[counts[kind] - 1])

    def rows_of(long_a, short_a, base, kind, back=False):
        pairs = [(long_a.at[0], at(base + shorts, shard))]
        pairs += [(short_a.at[i], at(base + i * short_len, short_len)) for i in range(slots)]
        return [move(kind, b, a) if back else move(kind, a, b) for a, b in pairs]

    in_x = rows_of(long_x, short_x, xs, "in")
    in_cols = move("in", proj.at[:, span(s * shard, shard)], pcols)
    in_wk = move("in", wk_in, at(weights + width, width))
    in_wv = move("in", wv_in, at(weights + 2 * width, width))
    in_wq = move("in", wq_in, at(weights, width))
    in_pshort = move("in", proj.at[:, pl.ds(0, short_len)], pshort)
    in_wo = move("in", wo_in, at(wo, width))
    in_up = [move("in", up_in.at[:, pl.ds(j * width, width)], at(up + j * width, width)) for j in range(4)]
    in_down = move("in", down_in, at(down, wide))
    for c in [in_x[0], in_cols] + in_x[1:] + [in_pshort, in_wk, in_wv, in_wq, in_wo] + in_up + [in_down]:
        c.start()
    greet(seq_peers() + grp_peers(groups))

    part, full = forward_exchange.part, forward_exchange.full
    blocks = KP // SEQ
    items = slots * KP
    in_x[0].wait()
    in_cols.wait()
    part[...] = mm(pcols[...], arena[window(xs + shorts, shard), :]).astype(BF).reshape(SEQ, blocks, width)
    forward_exchange.start()
    for c in in_x[1:] + [in_pshort]:
        c.wait()
    for i in range(slots):
        x = arena[window(xs + i * short_len, short_len), :]
        arena[window(y1 + i * KP, KP), :] = mm(pshort[...], x).astype(BF)
    in_wk.wait()

    def summaries(to, y, size):
        for n in range(2):
            w = arena[window(weights + (1 + n) * width, width), :]
            arena[window(to + n * size, size), :] = mm(arena[window(y, size), :], w).astype(BF)

    in_wv.wait()
    summaries(sums1, y1, items)
    forward_exchange.first()
    in_wq.wait()
    arena[window(q1, tokens), :] = (0.125 * mm(arena[window(xs, tokens), :], arena[window(weights, width), :])).astype(BF)
    out_q = move("out", at(q1, tokens), q_hbm)
    out_q.start()
    forward_exchange.second()
    heads = width // HD
    item_rows = heads * short_len // width * KP

    def head(h, size):
        beside = width // size
        return h // beside * KP, slice(h % beside * size, (h % beside + 1) * size)

    def staged(before, between, after):
        now, last = before(0), None
        for pair in range(heads // 2):
            ahead = before(pair + 1) if pair + 1 < heads // 2 else None
            middle = between(pair, *now)
            if last is not None:
                after(pair - 1, last)
            now, last = ahead, middle
        after(heads // 2 - 1, last)

    def lanes_of(pair):
        return slice(pair * 2 * HD, (pair + 1) * 2 * HD)

    def attend(row, size, ks, vs, probs):
        def scores(pair):
            q = arena[window(q1 + row, size, 128), lanes_of(pair)]
            return (mm(halves(arena[window(ks, KP), lanes_of(pair)]), q, 1, 1),)

        def softmax(pair, sc):
            parts = []
            for h in range(2):
                part = sc[h * KP : (h + 1) * KP]
                e = jnp.exp(part - jnp.max(part, 0, keepdims=True))
                parts.append((e * (1.0 / jnp.sum(e, 0, keepdims=True))).astype(BF))
                first, cols = head(2 * pair + h, size)
                arena[window(probs + first, KP, 128), cols] = parts[h]
            return jnp.concatenate(parts, 0)

        def mix(pair, p):
            out = mm(halves(arena[window(vs, KP), lanes_of(pair)]), p, 0, 0)
            arena[window(ms + row, size, 128), lanes_of(pair)] = out.T.astype(BF)

        staged(scores, softmax, mix)

    @pl.loop(0, slots)
    def _(i):
        attend(i * short_len, short_len, sums1 + i * KP, sums1 + (items + i * KP), probs1 + i * item_rows)

        @pl.when(i == 1)
        def _():
            forward_exchange.third()

    long_probs = probs1 + slots * item_rows
    out_probs = [move("out", at(probs1, slots * item_rows), probs_hbm.at[pl.ds(0, slots * item_rows)])]
    out_probs[0].start()
    forward_exchange.finish()
    long_sums = sums1 + 2 * items
    arena[window(y1 + items, KP), :] = full[...].reshape(KP, width)
    summaries(long_sums, y1 + items, KP)
    out_y = move("out", at(y1, items + KP), y_hbm)
    out_y.start()

    def enter(row, size, step):
        r = span(row, size, step)
        x = arena[window(xs + row, size, step), :].astype(F32)
        xh, rs = norm_stats(mm(arena[window(ms + row, size, step), :], arena[window(wo, width), :]) + x)
        arena[window(xhs + row, size, step), :] = xh.astype(BF)
        root[r, :] = jnp.broadcast_to(rs, (size, 128))
        hidden = xh * gain1 + shift1
        resid[r, :] = hidden
        arena[window(hs + row, size, step), :] = hidden.astype(BF)

    in_wo.wait()

    @pl.loop(0, slots // 2)
    def _(i):
        enter(i * 2 * short_len, 2 * short_len, 128)

    attend(shorts, shard, long_sums, long_sums + KP, long_probs)
    long_size = heads * shard // width * KP
    out_probs += [move("out", at(long_probs, long_size), probs_hbm.at[pl.ds(slots * item_rows, long_size)])]
    out_sums = move("out", at(sums1, (2 * slots + 2) * KP), sums_hbm)
    out_mixed = move("out", at(ms, tokens), mixed_hbm)
    for c in out_probs[1:] + [out_sums, out_mixed]:
        c.start()
    enter(shorts, shard, 128)
    block = tokens // 3
    in_dy = rows_of(long_dy, short_dy, xs, "in")
    for c in in_dy:
        c.start()
    for c in [out_y, out_q, out_mixed] + out_probs:
        c.wait()
    for c in in_up + [in_down]:
        c.wait()

    part_rows = tokens // 2

    @pl.loop(0, 8)
    def _(i):
        j, r = lax.div(i, 2), lax.rem(i, 2) * part_rows
        hidden = arena[window(hs + r, part_rows, 64), :]
        a, slope_j = gelu_pair(mm(hidden, arena[window(up + j * width, width, 128), :]))
        a = a.astype(BF)
        arena[window(act + j * tokens + r, part_rows, 64), :] = a
        arena[window(slope + j * tokens + r, part_rows, 64), :] = slope_j.astype(BF)
        resid[span(r, part_rows), :] += mm(a, arena[window(down + j * width, width, 128), :])

    vec[...] = jnp.zeros_like(vec)
    for c in in_dy:
        c.wait()
    rb = 128

    @pl.loop(0, tokens // rb)
    def _(i):
        r = span(i * rb, rb)
        rx = window(xs + i * rb, rb, 128)
        alive = jnp.where(lax.div(i * rb, short_len) < live[0], 1.0, 0.0).astype(F32)
        alive = jnp.where(i * rb >= shorts, 1.0, alive)
        xh, rs = norm_stats(resid[r, :])
        top = alive * arena[rx, :].astype(F32)
        vec[16:24, :] += fold_rows(top * xh)
        vec[24:32, :] += fold_rows(top)
        arena[rx, :] = (alive * (xh * gain2 + shift2)).astype(BF)
        dx = norm_back(top, gain2, xh, rs)
        resid[r, :] = dx
        arena[window(ms + i * rb, rb, 128), :] = dx.astype(BF)

    outs = rows_of(long_out, short_out, xs, "out", back=True)
    for c in outs:
        c.start()
    out_sums.wait()
    place = places(groups)

    def packed(base, order, value, step, first):
        for d in range(value.shape[0] // step):
            row, core = place[d][order]
            rows = slice(d * step + first, d * step + first + few)
            arena[window(base + row * 2 * few, 2 * few), core * lanes : (core + 1) * lanes] = jnp.concatenate(
                [value[rows, :lanes], value[rows, lanes:]], 0
            ).astype(BF)

    @pl.loop(0, groups)
    def _(j):
        value = mm(arena[window(act + j * tokens, tokens, 128), :], arena[window(ms, tokens), :], 0, 0)
        for n in range(4):
            packed(pack + n * width + j * 2 * few, n % 2, value, 4 * few, n * few)

    for piece in downs:
        piece.start()
    low = at(ms, tokens)

    @pl.loop(0, 8)
    def _(i):
        j, r = lax.div(i, 2), lax.rem(i, 2) * part_rows
        rj = window(slope + j * tokens + r, part_rows, 64)
        gb = low[span(r, part_rows), :]
        gu = mm(gb, arena[window(down + j * width, width, 128), :], 1, 1) * arena[rj, :].astype(F32)
        gu = gu.astype(BF)
        arena[rj, :] = gu
        resid[span(r, part_rows), :] += mm(gu, arena[window(up + j * width, width, 128), :], 1, 1)

        @pl.when(i == 0)
        def _():
            for piece in downs[:2]:
                piece.step(0)

        @pl.when(i == 1)
        def _():
            for piece in downs[2:]:
                piece.step(0)

        @pl.when(i == 4)
        def _():
            for piece in downs[:2]:
                piece.step(1)

    back = {}

    def load(name, a, b):
        back[name] = move("back", a, b)
        back[name].start()

    load("probs", probs_hbm, at(probs2, 4 * tokens))

    for piece in downs[2:]:
        piece.step(1)

    @pl.loop(0, 2)
    def _(m):
        for n in range(2):
            j = 2 * m + n
            gu = arena[window(slope + j * tokens, tokens, 128), :]
            packed(pack_up + j * width, n, mm(arena[window(hs, tokens), :], gu, 0, 0), few, 0)

        @pl.when(m == 0)
        def _():
            for piece in ups[:2]:
                piece.start()

        @pl.when(m == 1)
        def _():
            for piece in ups[2:]:
                piece.start()
            for piece in ups[:2]:
                piece.step(0)
            for piece in downs[:2]:
                piece.step(2)

    load("y", y_hbm, at(y2, items + KP))
    load("q", q_hbm, at(q2, tokens))
    load("mixed", mixed_hbm, at(ms2, tokens))
    for piece in downs[1:]:
        piece.hop(0).wait_send()
    load("sums", sums_hbm.at[pl.ds(0, 2 * items)], at(sums2, 2 * items))
    load("long_sums", sums_hbm.at[pl.ds(2 * items, 2 * KP)], at(long_sums2, 2 * KP))

    @pl.loop(0, tokens // rb)
    def _(i):
        r = span(i * rb, rb)
        gh = resid[r, :]
        xh = arena[window(xhs + i * rb, rb, 128), :].astype(F32)
        vec[0:8, :] += fold_rows(gh * xh)
        vec[8:16, :] += fold_rows(gh)
        dx = norm_back(gh, gain1, xh, root[r, 0:1])
        resid[r, :] = dx
        low[r, :] = dx.astype(BF)

    four = jnp.sum(vec[...].reshape(4, 8, width), 1)
    vectors.mine[0] = jnp.concatenate([four, jnp.zeros_like(four)], 0)
    vectors.start()
    for c in outs:
        c.wait()
    arena[window(xs, tokens), :] = mm(low[...], arena[window(wo, width), :], 1, 1).astype(BF)
    for piece in ups[2:]:
        piece.step(0)
    for piece in downs[2:]:
        piece.step(2)
    downs[0].hop(0).wait_send()
    back["mixed"].wait()
    packed(pack, 0, mm(arena[window(ms2, tokens), :], low[...], 0, 0), few, 0)
    unit_o.start()
    load("wq", wq_in, at(weights, width))
    load("wk", wk_in, at(weights + width, width))
    load("wv", wv_in, at(weights + 2 * width, width))
    for n, c in enumerate(rows_of(long_x, short_x, x2s, "back")):
        back["x", n] = c
        c.start()

    def attend_back(row, size, ks, vs, probs, n):
        def front(pair):
            gm = arena[window(xs + row, size, 128), lanes_of(pair)]
            p = []
            for h in range(2):
                first, cols = head(2 * pair + h, size)
                p.append(arena[window(probs + first, KP, 128), cols])
            gp = mm(halves(arena[window(vs, KP), lanes_of(pair)]), gm, 1, 1)
            grad = unhalve(mm(jnp.concatenate(p, 0), gm)).astype(BF)
            arena[window(value_grads + n * KP, KP, 128), lanes_of(pair)] = grad
            return gp, p

        def middle(pair, gp, p):
            parts = []
            for h in range(2):
                ph = p[h].astype(F32)
                t = ph * gp[h * KP : (h + 1) * KP]
                parts.append((t - ph * jnp.sum(t, 0, keepdims=True)).astype(BF))
            return jnp.concatenate(parts, 0)

        def rear(pair, gs):
            q = arena[window(q2 + row, size, 128), lanes_of(pair)]
            arena[window(key_grads + n * KP, KP, 128), lanes_of(pair)] = unhalve(mm(gs, q)).astype(BF)
            gq = mm(halves(arena[window(ks, KP), lanes_of(pair)]), gs, 0, 0).T.astype(BF).astype(F32)
            arena[window(gq2 + row, size, 128), lanes_of(pair)] = (gq * 0.125).astype(BF)

        staged(front, middle, rear)

    def through_projections(first, count):
        rows = count * KP
        key_grad = mm(arena[window(key_grads + first * KP, rows), :], arena[window(weights + width, width), :], 1, 1)
        return key_grad + mm(arena[window(value_grads + first * KP, rows), :], arena[window(weights + 2 * width, width), :], 1, 1)

    for name in ("q", "y", "sums", "long_sums", "probs"):
        back[name].wait()
    forward_exchange.close()
    attend_back(shorts, shard, long_sums2, long_sums2 + KP, probs2 + slots * item_rows, slots)
    unit_o.step(0)
    for name in ("wq", "wk", "wv"):
        back[name].wait()
    part[...] = through_projections(slots, 1).astype(BF).reshape(SEQ, blocks, width)
    backward_exchange.start()

    @pl.loop(0, slots)
    def _(i):
        attend_back(i * short_len, short_len, sums2 + i * KP, sums2 + (items + i * KP), probs2 + i * item_rows, i)

        @pl.when(i == 0)
        def _():
            backward_exchange.first()
            for piece in ups[:2]:
                piece.step(1)

        @pl.when(i == 1)
        def _():
            vectors.step(0)
            for piece in ups[2:]:
                piece.step(1)

        @pl.when(i == slots - 1)
        def _():
            backward_exchange.second()
            for piece in ups[:2]:
                piece.step(2)

    for n in range(1 + slots):
        back["x", n].wait()
    x2, gq = at(x2s, tokens), at(gq2, tokens)

    packed(pack + width, 1, mm(x2[...], gq[...], 0, 0), few, 0)
    unit_q.start()
    unit_o.step(1)
    y = arena[window(y2, items + KP), :]
    packed(pack + 2 * width, 0, mm(y, arena[window(value_grads, items + KP), :], 0, 0), few, 0)
    unit_v.start()
    vectors.step(1)
    unit_q.step(0)
    packed(pack + 3 * width, 1, mm(y, arena[window(key_grads, items + KP), :], 0, 0), few, 0)
    unit_k.start()
    unit_v.step(0)
    backward_exchange.third()
    for piece in ups[2:]:
        piece.step(2)

    arena[window(through, items), :] = through_projections(0, slots).astype(BF)
    unit_k.step(0)
    unit_o.step(2)
    pacc[...] = jnp.zeros_like(pacc)

    def leave(cols, row, size, n):
        grad = arena[window(through + n * KP, KP), :]
        r = span(row, size, 128)
        dx = resid[r, :] + mm(gq[r, :], arena[window(weights, width), :], 1, 1) + mm(cols[...], grad, 0, 0)
        arena[window(xs + row, size, 128), :] = dx.astype(BF)
        return mm(grad, x2[r, :], 1, 1)

    @pl.loop(0, slots)
    def _(i):
        pacc[...] += leave(pshort, i * short_len, short_len, i)

    prow = KP // groups
    projected.part[:, :, shard:] = pacc[...].astype(BF).reshape(groups, prow, short_len)
    projected.start(shard, short_len)
    backward_exchange.finish()
    arena[window(through + items, KP), :] = full[...].reshape(KP, width)
    long_cols = leave(pcols, shorts, shard, slots)
    projected.part[:, :, 0:shard] = long_cols.astype(BF).reshape(groups, prow, shard)
    projected.start(0, shard)
    unit_q.step(1)
    vectors.step(2)
    outs = rows_of(long_grad, short_grad, xs, "out", back=True)
    for c in outs:
        c.start()
    unit_v.step(1)
    projected.across_all(shard, short_len)
    for n, piece in enumerate(downs):
        piece.total(grad_down, n * few, 0)
    for n, piece in enumerate(ups):
        piece.total(grad_up, 0, n * width)
    unit_o.total(grad_o, 0, 0)
    unit_k.step(1)
    unit_q.step(2)
    vec_out[...] = vectors.total()
    unit_v.step(2)
    projected.finish(grad_proj, shard)
    unit_k.step(2)
    unit_q.total(grad_q, 0, 0)
    unit_v.total(grad_v, 0, 0)
    unit_k.total(grad_k, 0, 0)
    for c in outs:
        c.wait()
    for piece in downs:
        for n in range(1, 3):
            piece.hop(n).wait_send()
        for c in piece.along():
            c.wait_send()
    for piece in ups + [unit_o, unit_q, unit_v, unit_k, vectors, projected, backward_exchange]:
        piece.close()


def fast_shards(groups, *args):
    (long_x, short_x, long_dy, short_dy, live, wq, wk, wv, wo, up, down, proj, g1, b1, g2, b2) = args
    slots, short_len, width = short_x.shape
    shard = long_x.shape[1]
    tokens = slots * short_len + shard
    wide = up.shape[1]
    devices = groups * SEQ
    few = width // devices
    sds = jax.ShapeDtypeStruct
    anyspace = pl.BlockSpec(memory_space=pl.ANY)
    vmem = pl.BlockSpec(memory_space=pltpu.VMEM)
    dma = pltpu.SemaphoreType.DMA
    prow = KP // groups
    out_shapes = [sds(a.shape, BF) for a in (long_x, short_x, long_x, short_x)]
    grads = [(few, width)] * 4 + [(few, wide), (4 * few, width), (prow, shard), (8, width)]
    out_shapes += [sds(a, F32) for a in grads]
    row = (tokens, width)
    out_shapes += [
        sds(a, BF)
        for a in [row, ((slots + 1) * KP, width), row, (4 * tokens, width), ((2 * slots + 2) * KP, width)]
    ]
    regions = [4 * tokens, 4 * tokens, 2 * wide, tokens, tokens, 2 * tokens, width, 4 * width, (slots + 1) * KP]
    heads = short_len // shard
    scratch = [
        *[pltpu.VMEM((n, width), BF) for n in regions],
        pltpu.VMEM(row, F32),
        pltpu.VMEM((tokens, 128), F32),
        pltpu.VMEM((32, width), F32),
        pltpu.VMEM((KP, shard), BF),
        pltpu.VMEM((KP, short_len), BF),
        pltpu.VMEM((KP, short_len), F32),
        dma((12 + 2 * (1 + slots),)),
        dma((13 + 2 * (1 + slots),)),
        dma((13 + 1 + slots,)),
    ]
    scratch += exchange_scratch(KP // SEQ, width)
    along = [dma((groups - 1,)), dma((groups - 1,))]
    scratch += [pltpu.VMEM((n, 8, width), F32) for n in (4, 3, groups - 1)] + [dma((3,)), dma((3,))] + along
    scratch += [pltpu.VMEM((n, prow, shard + short_len), BF) for n in (groups, groups - 1)]
    scratch += [pltpu.VMEM((n, prow, shard), BF) for n in (heads, SEQ - 1)]
    scratch += along + along + [dma((heads,)), dma((SEQ - 1,))]
    lanes = width // 2
    unit = [pltpu.VMEM((width // n, lanes), BF) for n in (1, 2, 4)]
    unit += [pltpu.VMEM((groups - 1, 2 * few, lanes), BF), dma((3,)), dma((3,))] + along
    scratch += unit * 12
    outs = pl.pallas_call(
        functools.partial(layer_kernel, slots, groups, shard),
        name="encoder_layer",
        out_shape=out_shapes,
        in_specs=[anyspace] * 4 + [pl.BlockSpec(memory_space=pltpu.SMEM)] + [anyspace] * 7 + [vmem] * 4,
        out_specs=[anyspace] * 4 + [vmem] * 8 + [anyspace] * 5,
        scratch_shapes=scratch,
        compiler_params=pltpu.CompilerParams(
            collective_id=0, has_side_effects=True, vmem_limit_bytes=VMEM_BYTES
        ),
    )(long_x, short_x, long_dy, short_dy, live, wq, wk, wv, wo, up, down, proj, g1, b1, g2, b2)
    return emit_call(outs[:12], few)


def emit_kernel(*refs):
    *ins, vec = refs[:12]
    outs, vectors, stages = refs[12:23], refs[23:27], refs[27:38]
    sem_in, sem_out = refs[38:]
    reads = [pltpu.make_async_copy(a, b, sem_in.at[n]) for n, (a, b) in enumerate(zip(ins, stages))]
    writes = [pltpu.make_async_copy(a, b, sem_out.at[n]) for n, (a, b) in enumerate(zip(stages, outs))]
    for c in reads:
        c.start()
    g, s = here()
    width = vec.shape[1]
    few = vectors[0].shape[0]
    mine = pltpu.roll(vec[...], width - (g * SEQ + s) * few, 1)
    for n in range(4):
        vectors[n][...] = mine[n, 0:few]
    for a, b in zip(reads, writes):
        a.wait()
        b.start()
    for c in writes:
        c.wait()


def emit_call(arrays, few):
    anyspace = pl.BlockSpec(memory_space=pl.ANY)
    vmem = pl.BlockSpec(memory_space=pltpu.VMEM)
    return pl.pallas_call(
        emit_kernel,
        name="emit",
        out_shape=[jax.ShapeDtypeStruct(a.shape, a.dtype) for a in arrays[:11]] + [jax.ShapeDtypeStruct((few,), F32)] * 4,
        in_specs=[anyspace] * 11 + [vmem],
        out_specs=[anyspace] * 11 + [vmem] * 4,
        scratch_shapes=[pltpu.VMEM(a.shape, a.dtype) for a in arrays[:11]] + [pltpu.SemaphoreType.DMA((11,))] * 2,
        compiler_params=pltpu.CompilerParams(vmem_limit_bytes=VMEM_BYTES),
    )(*arrays)


def fits(mesh, args):
    long_x, width, wide = args[0], args[0].shape[2], args[9].shape[1]
    devices = mesh.shape["grp"] * mesh.shape["seq"]
    whole = width % (devices * 8) == 0 and wide == 4 * width
    return mesh.shape["seq"] == SEQ and whole and long_x.shape[0] == 1


def solution(mesh):
    placed = (
        P("grp", "seq", None),
        P(("grp", "seq"), None, None),
        P("grp", "seq", None),
        P(("grp", "seq"), None, None),
        P(("grp", "seq")),
        P(),
        P(),
        P(),
        P(),
        P(),
        P(),
        P(),
        P(),
        P(),
        P(),
        P(),
    )
    groups = mesh.shape["grp"]

    def body(*args):
        if fits(mesh, args):
            return fast_shards(groups, *args)
        return shards(*args)

    return jax.shard_map(
        body,
        mesh=mesh,
        in_specs=placed,
        out_specs=(
            P("grp", "seq", None),
            P(("grp", "seq"), None, None),
            P("grp", "seq", None),
            P(("grp", "seq"), None, None),
            P(("grp", "seq"), None),
            P(("grp", "seq"), None),
            P(("grp", "seq"), None),
            P(("grp", "seq"), None),
            P(("grp", "seq"), None),
            P(("grp", "seq"), None),
            P("grp", "seq"),
            P(("grp", "seq")),
            P(("grp", "seq")),
            P(("grp", "seq")),
            P(("grp", "seq")),
        ),
        check_vma=False,
    )
```

profile of v0, /device:TPU:0, one launch (start us, length us, event | category | flops | bytes accessed | tf_op | source)
XLA Modules:
  0.0 150.8 jit_solution(6698156672065359499)
XLA Ops:
  1.3 144.3 %encoder_layer.1 = (bf16[1,128,768]{2,1,0:T(8,128)(2,1)}, bf16[4,256,768]{2,1,0:T(8,128)(2,1)}, bf16[1,128,768]{2,1,0:T(8,128)(2,1)}, bf16[4,256,768]{2,1,0:T(8,...) custom-call(bf16[1,128,768]{2,1,0:T(8,128)(2,1)} %refs_0_.1, ...), custom_call_target="tpu_custom_call" | custom-call | tf_op jit(solution)/shard_map/encoder_layer/pallas_call | solution.py:1227
  145.6 5.0 %emit.1 = (bf16[1,128,768]{2,1,0:T(8,128)(2,1)}, bf16[4,256,768]{2,1,0:T(8,128)(2,1)}, bf16[1,128,768]{2,1,0:T(8,128)(2,1)}, bf16[4,256,768]{2,1,0:T(8,128)(2,1)...) custom-call(bf16[1,128,768]{2,1,0:T(8,128)(2,1)} %get-tuple-element., ...), custom_call_target="tpu_custom_call" | custom-call | tf_op jit(solution)/shard_map/emit/pallas_call | solution.py:1265
where the time goes:
time: 151 us
  Pallas kernels  149 us (99%)
  between operations  1.51 us (1%)
    pallas_call x1, Pallas kernels, fast_shards(): pl.pallas_call(functools.partial(layer_kernel, slots, groups, shard), nam...  144 us
    pallas_call x1, Pallas kernels, emit_call(): pl.pallas_call(emit_kernel, name='emit', out_shape=[jax.ShapeDtypeStruct(...  5.02 us

commit v1 on v0

--- a/solution.py
+++ b/solution.py
@@ -886,17 +886,35 @@
     for c in in_up + [in_down]:
         c.wait()
 
-    part_rows = tokens // 2
-
-    @pl.loop(0, 8)
-    def _(i):
-        j, r = lax.div(i, 2), lax.rem(i, 2) * part_rows
-        hidden = arena[window(hs + r, part_rows, 64), :]
-        a, slope_j = gelu_pair(mm(hidden, arena[window(up + j * width, width, 128), :]))
-        a = a.astype(BF)
-        arena[window(act + j * tokens + r, part_rows, 64), :] = a
-        arena[window(slope + j * tokens + r, part_rows, 64), :] = slope_j.astype(BF)
-        resid[span(r, part_rows), :] += mm(a, arena[window(down + j * width, width, 128), :])
+    part_rows = tokens // 3
+
+    def rows_in(place, j, r):
+        return window(place + (j * tokens + r * part_rows), part_rows, 64)
+
+    @pl.loop(0, 4)
+    def _(j):
+        def upward(r):
+            return mm(arena[rows_in(hs, 0, r), :], arena[window(up + j * width, width, 128), :])
+
+        def activate(r, u):
+            a, slope_j = gelu_pair(u)
+            a = a.astype(BF)
+            arena[rows_in(act, j, r), :] = a
+            arena[rows_in(slope, j, r), :] = slope_j.astype(BF)
+            return a
+
+        def downward(r, a):
+            resid[pl.ds(r * part_rows, part_rows), :] += mm(a, arena[window(down + j * width, width, 128), :])
+
+        u0 = upward(0)
+        u1 = upward(1)
+        a0 = activate(0, u0)
+        u2 = upward(2)
+        a1 = activate(1, u1)
+        downward(0, a0)
+        a2 = activate(2, u2)
+        downward(1, a1)
+        downward(2, a2)
 
     vec[...] = jnp.zeros_like(vec)
     for c in in_dy:
@@ -942,31 +960,35 @@
         piece.start()
     low = at(ms, tokens)
 
-    @pl.loop(0, 8)
-    def _(i):
-        j, r = lax.div(i, 2), lax.rem(i, 2) * part_rows
-        rj = window(slope + j * tokens + r, part_rows, 64)
-        gb = low[span(r, part_rows), :]
-        gu = mm(gb, arena[window(down + j * width, width, 128), :], 1, 1) * arena[rj, :].astype(F32)
-        gu = gu.astype(BF)
-        arena[rj, :] = gu
-        resid[span(r, part_rows), :] += mm(gu, arena[window(up + j * width, width, 128), :], 1, 1)
-
-        @pl.when(i == 0)
+    @pl.loop(0, 4)
+    def _(j):
+        def grad_up_of(r):
+            gb = low[pl.ds(r * part_rows, part_rows), :]
+            gu = mm(gb, arena[window(down + j * width, width, 128), :], 1, 1)
+            gu = (gu * arena[rows_in(slope, j, r), :].astype(F32)).astype(BF)
+            arena[rows_in(slope, j, r), :] = gu
+            return gu
+
+        def into_resid(r, gu):
+            resid[pl.ds(r * part_rows, part_rows), :] += mm(gu, arena[window(up + j * width, width, 128), :], 1, 1)
+
+        gu0 = grad_up_of(0)
+        gu1 = grad_up_of(1)
+        into_resid(0, gu0)
+        gu2 = grad_up_of(2)
+        into_resid(1, gu1)
+        into_resid(2, gu2)
+
+        @pl.when(j == 0)
         def _():
             for piece in downs[:2]:
                 piece.step(0)
 
-        @pl.when(i == 1)
+        @pl.when(j == 1)
         def _():
             for piece in downs[2:]:
                 piece.step(0)
 
-        @pl.when(i == 4)
-        def _():
-            for piece in downs[:2]:
-                piece.step(1)
-
     back = {}
 
     def load(name, a, b):
@@ -975,7 +997,7 @@
 
     load("probs", probs_hbm, at(probs2, 4 * tokens))
 
-    for piece in downs[2:]:
+    for piece in downs:
         piece.step(1)
 
     @pl.loop(0, 2)

time: 151 us -> 148 us (0.980)
  Pallas kernels: 149 us -> 146 us
    pallas_call x1, Pallas kernels: 144 us -> 141 us  [fast_shards(): pl.pallas_call(functools.partial(layer_kernel, slots, groups, shard), nam...]
where the time goes in v1:
time: 148 us
  Pallas kernels  146 us (99%)
  between operations  1.51 us (1%)
    pallas_call x1, Pallas kernels, fast_shards(): pl.pallas_call(functools.partial(layer_kernel, slots, groups, shard), nam...  141 us
    pallas_call x1, Pallas kernels, emit_call(): pl.pallas_call(emit_kernel, name='emit', out_shape=[jax.ShapeDtypeStruct(...  5.02 us

profile of v1, /device:TPU:0, one launch (start us, length us, event | category | flops | bytes accessed | tf_op | source)
XLA Modules:
  0.0 148.0 jit_solution(11982020275813263234)
XLA Ops:
  1.3 141.5 %encoder_layer.1 = (bf16[1,128,768]{2,1,0:T(8,128)(2,1)}, bf16[4,256,768]{2,1,0:T(8,128)(2,1)}, bf16[1,128,768]{2,1,0:T(8,128)(2,1)}, bf16[4,256,768]{2,1,0:T(8,...) custom-call(bf16[1,128,768]{2,1,0:T(8,128)(2,1)} %refs_0_.1, ...), custom_call_target="tpu_custom_call" | custom-call | tf_op jit(solution)/shard_map/encoder_layer/pallas_call | solution.py:1249
  142.8 5.0 %emit.1 = (bf16[1,128,768]{2,1,0:T(8,128)(2,1)}, bf16[4,256,768]{2,1,0:T(8,128)(2,1)}, bf16[1,128,768]{2,1,0:T(8,128)(2,1)}, bf16[4,256,768]{2,1,0:T(8,128)(2,1)...) custom-call(bf16[1,128,768]{2,1,0:T(8,128)(2,1)} %get-tuple-element., ...), custom_call_target="tpu_custom_call" | custom-call | tf_op jit(solution)/shard_map/emit/pallas_call | solution.py:1287

commit v2 on v1

--- a/solution.py
+++ b/solution.py
@@ -997,7 +997,7 @@
 
     load("probs", probs_hbm, at(probs2, 4 * tokens))
 
-    for piece in downs:
+    for piece in downs[:2]:
         piece.step(1)
 
     @pl.loop(0, 2)
@@ -1011,6 +1011,8 @@
         def _():
             for piece in ups[:2]:
                 piece.start()
+            for piece in downs[2:]:
+                piece.step(1)
 
         @pl.when(m == 1)
         def _():
@@ -1018,8 +1020,6 @@
                 piece.start()
             for piece in ups[:2]:
                 piece.step(0)
-            for piece in downs[:2]:
-                piece.step(2)
 
     load("y", y_hbm, at(y2, items + KP))
     load("q", q_hbm, at(q2, tokens))
@@ -1040,6 +1040,8 @@
         resid[r, :] = dx
         low[r, :] = dx.astype(BF)
 
+    for piece in downs[:2]:
+        piece.step(2)
     four = jnp.sum(vec[...].reshape(4, 8, width), 1)
     vectors.mine[0] = jnp.concatenate([four, jnp.zeros_like(four)], 0)
     vectors.start()

time: 148 us -> 146 us (0.986)
  Pallas kernels: 146 us -> 144 us
    pallas_call x1, Pallas kernels: 141 us -> 139 us  [fast_shards(): pl.pallas_call(functools.partial(layer_kernel, slots, groups, shard), nam...]
where the time goes in v2:
time: 146 us
  Pallas kernels  144 us (99%)
  between operations  1.51 us (1%)
    pallas_call x1, Pallas kernels, fast_shards(): pl.pallas_call(functools.partial(layer_kernel, slots, groups, shard), nam...  139 us
    pallas_call x1, Pallas kernels, emit_call(): pl.pallas_call(emit_kernel, name='emit', out_shape=[jax.ShapeDtypeStruct(...  5.02 us

profile of v2, /device:TPU:0, one launch (start us, length us, event | category | flops | bytes accessed | tf_op | source)
XLA Modules:
  0.0 145.6 jit_solution(16722700361590486589)
XLA Ops:
  1.3 139.1 %encoder_layer.1 = (bf16[1,128,768]{2,1,0:T(8,128)(2,1)}, bf16[4,256,768]{2,1,0:T(8,128)(2,1)}, bf16[1,128,768]{2,1,0:T(8,128)(2,1)}, bf16[4,256,768]{2,1,0:T(8,...) custom-call(bf16[1,128,768]{2,1,0:T(8,128)(2,1)} %refs_0_.1, ...), custom_call_target="tpu_custom_call" | custom-call | tf_op jit(solution)/shard_map/encoder_layer/pallas_call | solution.py:1251
  140.4 5.0 %emit.1 = (bf16[1,128,768]{2,1,0:T(8,128)(2,1)}, bf16[4,256,768]{2,1,0:T(8,128)(2,1)}, bf16[1,128,768]{2,1,0:T(8,128)(2,1)}, bf16[4,256,768]{2,1,0:T(8,128)(2,1)...) custom-call(bf16[1,128,768]{2,1,0:T(8,128)(2,1)} %get-tuple-element., ...), custom_call_target="tpu_custom_call" | custom-call | tf_op jit(solution)/shard_map/emit/pallas_call | solution.py:1289
